TPU v7x, 32 devices: a whole 2x2x4 slice. The times are simulated.
32 devices in a mesh: dp: 8 (over z, core), ctx: 4 (over y, x).
Axes of the slice: x: 2, y: 2, z: 4, core: 2. Of those that a mesh axis runs over, the one named last changes fastest.
Arguments:
- hidden: bfloat16 [8, 512, 4096], P('dp', 'ctx'), may hold values from -6 to 6
- queries: bfloat16 [8, 512, 4096], P('dp', 'ctx'), may hold values from -6 to 6
- keys: bfloat16 [8, 512, 256], P('dp', 'ctx'), may hold values from -6 to 6
- values: bfloat16 [8, 512, 256], P('dp', 'ctx'), may hold values from -24 to 24
- out_weight: bfloat16 [4096, 4096], P(None, 'ctx'), may hold values from -0.09375 to 0.09375
- norm_gain: float32 [4096], replicated, may hold values from 0.1 to 1.9
- routes: int32 [8, 512, 8], P('dp', 'ctx'), may hold values from 0 to 31, all different within a row; in each aligned block of 128 rows (0 to 127, 128 to 255, ..., all dimensions but the last counted through in order) at most 36 rows name the same one
- slot_scores: float32 [8, 512, 8], P('dp', 'ctx'), may hold values from 0.1 to 1
- gate_weight: bfloat16 [32, 4096, 768], P(('dp', 'ctx')), may hold values from -0.09375 to 0.09375
- up_weight: bfloat16 [32, 4096, 768], P(('dp', 'ctx')), may hold values from -0.09375 to 0.09375
- down_weight: bfloat16 [32, 768, 4096], P(('dp', 'ctx')), may hold values from -0.21875 to 0.21875
Outputs:
- output: bfloat16 [8, 512, 4096], P('dp', 'ctx')
Inputs may be any that keep to these rules, and one draw needn't show every extreme that they name: In each aligned block of 128 tokens (the tokens of one device, sequences in order) no expert is named by more than 36 of the block's routes, a bound that some block reaches.
All inputs are finite; a program needn't handle non-finite values.
Results may differ from a plain program's by a relative error of at most 0.0065.
Values may be sent and summed in bfloat16 or wider, within the bound.
A program may use at most 192 MiB of HBM per device.

v0:
```python
import jax
import jax.numpy as jnp
from jax import lax
from jax.sharding import PartitionSpec as P

HQ = 32
KVH = 2
DH = 128
TOP = 8


def expert_ffn(slots_in, w_gate, w_up, w_down):
    flat_rows = slots_in.reshape(-1, slots_in.shape[-1])
    gated = jnp.dot(flat_rows, w_gate, preferred_element_type=jnp.float32)
    lifted = jnp.dot(flat_rows, w_up, preferred_element_type=jnp.float32)
    activated = (jax.nn.silu(gated) * lifted).astype(jnp.bfloat16)
    result = jnp.dot(activated, w_down, preferred_element_type=jnp.float32).astype(jnp.bfloat16)
    return result.reshape(slots_in.shape)


def local(
    hidden,
    queries,
    keys,
    values,
    out_weight,
    norm_gain,
    routes,
    slot_scores,
    gate_weight,
    up_weight,
    down_weight,
):
    tok_count = hidden.shape[1]
    model_width = hidden.shape[2]
    group_size = HQ // KVH
    score_scale = DH ** (-0.5)
    ctx_index = lax.axis_index("ctx")
    query_rows = queries[0].reshape(tok_count, KVH, group_size, DH)
    query_pos = ctx_index * tok_count + jnp.arange(tok_count, dtype=jnp.int32)
    key_piece = lax.all_gather(keys, "ctx", axis=1, tiled=True)
    value_piece = lax.all_gather(values, "ctx", axis=1, tiled=True)
    key_count = key_piece.shape[1]
    key_rows = key_piece[0].reshape(key_count, KVH, DH)
    value_rows = value_piece[0].reshape(key_count, KVH, DH)
    key_pos = jnp.arange(key_count, dtype=jnp.int32)
    running_max = jnp.full((KVH, group_size, tok_count), -1e30, jnp.float32)
    scores = (
        jnp.einsum("qkgd,jkd->kgqj", query_rows, key_rows, preferred_element_type=jnp.float32)
        * score_scale
    )
    causal = key_pos[None, :] <= query_pos[:, None]
    scores = jnp.where(causal, scores, -1e30)
    new_max = jnp.maximum(running_max, jnp.max(scores, axis=-1))
    weights = jnp.where(causal, jnp.exp(scores - new_max[..., None]), 0.0)
    running_sum = jnp.sum(weights, axis=-1)
    numerator = jnp.einsum(
        "kgqj,jkd->kgqd",
        weights.astype(jnp.bfloat16),
        value_rows,
        preferred_element_type=jnp.float32,
    )
    running_max, running_sum, numerator = (new_max, running_sum, numerator)
    attended = numerator / running_sum[..., None]
    attended = (
        jnp.transpose(attended, (2, 0, 1, 3)).reshape(tok_count, HQ * DH).astype(jnp.bfloat16)
    )
    columns = jnp.dot(
        lax.all_gather(attended, "ctx", axis=0, tiled=True),
        out_weight,
        preferred_element_type=jnp.float32,
    ).astype(jnp.bfloat16)
    projected = lax.all_to_all(columns, "ctx", split_axis=0, concat_axis=1, tiled=True)
    residual = hidden[0].astype(jnp.float32) + projected.astype(jnp.float32)
    normed = (
        residual
        * lax.rsqrt(jnp.mean(residual * residual, axis=1, keepdims=True) + 1e-06)
        * norm_gain
    ).astype(jnp.bfloat16)
    score_rows = slot_scores[0]
    slot_gates = score_rows / jnp.sum(score_rows, axis=1, keepdims=True)
    expert_total = lax.axis_size(("dp", "ctx"))
    capacity = max(2, tok_count * TOP * 9 // (8 * expert_total))
    expert_ids = routes[0].reshape(tok_count * TOP)
    one_hot = (expert_ids[:, None] == jnp.arange(expert_total, dtype=jnp.int32)[None, :]).astype(
        jnp.int32
    )
    earlier = jnp.sum((jnp.cumsum(one_hot, axis=0) - one_hot) * one_hot, axis=1)
    slot_index = expert_ids * capacity + earlier
    token_of = jnp.arange(tok_count * TOP, dtype=jnp.int32) // TOP
    outgoing = (
        jnp.zeros((expert_total * capacity, model_width), jnp.bfloat16)
        .at[slot_index]
        .set(normed[token_of])
    )
    outgoing = outgoing.reshape(expert_total, capacity, model_width)
    served = expert_ffn(
        lax.all_to_all(outgoing, ("dp", "ctx"), split_axis=0, concat_axis=0, tiled=True),
        gate_weight[0],
        up_weight[0],
        down_weight[0],
    )
    returned = lax.all_to_all(served, ("dp", "ctx"), split_axis=0, concat_axis=0, tiled=True)
    returned = returned.reshape(expert_total * capacity, model_width)
    picked = returned[slot_index].reshape(tok_count, TOP, model_width)
    mixture = jnp.sum(slot_gates[:, :, None] * picked.astype(jnp.float32), axis=1)
    return (residual + mixture).astype(jnp.bfloat16)[None]


def solution(mesh):
    return jax.shard_map(
        local,
        mesh=mesh,
        in_specs=(
            P("dp", "ctx", None),
            P("dp", "ctx", None),
            P("dp", "ctx", None),
            P("dp", "ctx", None),
            P(None, "ctx"),
            P(),
            P("dp", "ctx", None),
            P("dp", "ctx", None),
            P(("dp", "ctx"), None, None),
            P(("dp", "ctx"), None, None),
            P(("dp", "ctx"), None, None),
        ),
        out_specs=P("dp", "ctx", None),
        check_vma=False,
    )
```

profile of v0, /device:TPU:0, one launch (start us, length us, event | category | flops | bytes accessed | tf_op | source)
XLA Modules:
  0.0 747.8 jit_solution(6065845563719159171)
XLA Ops:
  6.5 10.7 %all_gather.10 = bf16[1,512,256]{2,1,0:T(8,128)(2,1)S(1)} all-gather(bf16[1,128,256]{2,1,0:T(8,128)(2,1)} %param.14), channel_id=1, replica_groups=mesh['dp'=8,'ctx'=4] {'ctx'}, dimensions={1}, use_global_device_ids=true | all-gather | bytes 327680 | tf_op jit(solution)/shard_map/all_gather | solution.py:42
  17.5 1.0 copy.18
  18.4 8.7 %all_gather.9 = bf16[1,512,256]{1,2,0:T(8,128)(2,1)S(1)} all-gather(bf16[1,128,256]{1,2,0:T(8,128)(2,1)S(1)} %copy.18), channel_id=1, replica_groups=mesh['dp'=8,'ctx'=4] {'ctx'}, dimensions={1}, use_global_device_ids=true | all-gather | bytes 327680 | tf_op jit(solution)/shard_map/all_gather | solution.py:41
  27.1 1.5 copy.37
  28.6 2.1 fusion.1
  30.7 2.1 fusion.7
  32.8 3.2 fusion.23
  36.5 9.0 %reduce-window.6 = s32[32,8,128]{2,1,0:T(8,128)S(1)} reduce-window(s32[32,8,128]{2,1,0:T(8,128)S(1)} %fusion.31, s32[]{:T(128)} %constant.45.clone.1), window={size=1x1x128 pad=0_0x0_0x127_0}, to_apply=%region_3.4 | reduce-window | flops 4161536 | bytes 262148 | tf_op jit(solution)/shard_map/reduce-window
  45.9 43.1 %all-gather.2.cloned.1.call-done = bf16[512,4096]{0,1:T(8,128)(2,1)} async-done(((bf16[128,4096]{0,1:T(8,128)(2,1)}), bf16[512,4096]{0,1:T(8,128)(2,1)}) %all-gather.2.cloned.1.call-update) | async-done | bytes 4194320 | tf_op jit(solution)/shard_map/all_gather | solution.py:69
  89.0 10.1 %convolution_convert_fusion.1 = bf16[512,1024]{1,0:T(8,128)(2,1)} fusion(bf16[512,4096]{0,1:T(8,128)(2,1)} %all-gather.2.cloned.1.call-done, bf16[4096,1024]{1,0:T(8,128)(2,1)} %param.15), kind=kOutput, calls=%fused_computation.33 | convolution fusion | flops 4295491584 | bytes 13631488 | tf_op jit(solution)/shard_map/dot_general | solution.py:68
  99.1 3.8 all-to-all-start
  103.2 13.7 %all-to-all-done = bf16[4,128,1024]{2,1,0:T(8,128)(2,1)S(1)} async-done(((bf16[4,128,1024]{2,1,0:T(8,128)(2,1)}), bf16[4,128,1024]{2,1,0:T(8,128)(2,1)S(1)}, u32[]{:S(2)}, u32[]{:S(2)}) %all-to-all-start) | async-done | bytes 1048608 | tf_op jit(solution)/shard_map/all_to_all | solution.py:73
  116.8 1.6 convert_bitcast_fusion
  118.7 0.4 multiply_reduce_fusion
  119.2 0.4 multiply_convert_fusion
  119.6 7.7 %gather_fusion = bf16[1024,4096]{1,0:T(8,128)(2,1)} fusion(bf16[128,4096]{1,0:T(8,128)(2,1)S(1)} %multiply_convert_fusion, s32[1024]{0:T(1024)S(1)} %broadcast_clamp_fusion.1), kind=kCustom, calls=%fused_computation | custom fusion | bytes 16781312 | tf_op jit(solution)/shard_map/gather | solution.py:94
  127.3 18.4 %scatter_custom_fusion = bf16[1152,4096]{1,0:T(8,128)(2,1)} fusion(s32[1024]{0:T(1024)S(1)} %bitcast.106, bf16[1024,4096]{1,0:T(8,128)(2,1)} %gather_fusion, bf16[]{:T(256)} %constant.43.clone.1), kind=kCustom, calls=%fused_computation.16 | custom fusion | bytes 9437696 | tf_op jit(solution)/shard_map/scatter | solution.py:94
  145.7 13.2 %reshape.163 = bf16[32,36,4096]{2,1,0:T(8,128)(2,1)} reshape(bf16[1152,4096]{1,0:T(8,128)(2,1)} %scatter_custom_fusion) | data formatting | bytes 18874368 | tf_op jit(solution)/shard_map/reshape | solution.py:96
  158.9 233.5 %all_to_all.23 = bf16[32,36,4096]{2,1,0:T(8,128)(2,1)} all-to-all(bf16[32,36,4096]{2,1,0:T(8,128)(2,1)} %reshape.163), channel_id=1, replica_groups=mesh['dp'=8,'ctx'=4] {'dp','ctx'}, dimensions={0} | all-to-all | bytes 18874368 | tf_op jit(solution)/shard_map/all_to_all | solution.py:98
  392.4 13.3 %reshape.164 = bf16[1152,4096]{1,0:T(8,128)(2,1)} reshape(bf16[32,36,4096]{2,1,0:T(8,128)(2,1)} %all_to_all.23) | data formatting | bytes 18874368 | tf_op jit(solution)/shard_map/reshape | solution.py:13
  405.7 12.0 %fusion.5 = f32[1152,768]{1,0:T(8,128)S(1)} fusion(bf16[1152,4096]{1,0:T(8,128)(2,1)} %reshape.164, bf16[1,4096,768]{2,1,0:T(8,128)(2,1)} %param.19), kind=kOutput, calls=%fused_computation.12 | convolution fusion | flops 7247757312 | bytes 19267584 | tf_op jit(solution)/shard_map/dot_general | solution.py:14
  417.7 10.3 %fusion.17 = bf16[1152,768]{1,0:T(8,128)(2,1)S(1)} fusion(bf16[1152,4096]{1,0:T(8,128)(2,1)S(1)} %copy-done, bf16[1,4096,768]{2,1,0:T(8,128)(2,1)} %param.20, f32[1152,768]{1,0:T(8,128)S(1)} %fusion.5), kind=kOutput, calls=%fused_computation.21 | convolution fusion | flops 7253065728 | bytes 21037056 | tf_op jit(solution)/shard_map/dot_general | solution.py:15
  428.0 9.6 %convolution_convert_fusion = bf16[1152,4096]{1,0:T(8,128)(2,1)} fusion(bf16[1152,768]{1,0:T(8,128)(2,1)S(1)} %fusion.17, bf16[1,768,4096]{2,1,0:T(8,128)(2,1)S(1)} %bitcast.110), kind=kOutput, calls=%fused_computation.5 | convolution fusion | flops 7252475904 | bytes 17498112 | tf_op jit(solution)/shard_map/dot_general | solution.py:17
  437.6 13.1 %reshape.165 = bf16[32,36,4096]{2,1,0:T(8,128)(2,1)} reshape(bf16[1152,4096]{1,0:T(8,128)(2,1)} %convolution_convert_fusion) | data formatting | bytes 18874368 | tf_op jit(solution)/shard_map/reshape | solution.py:18
  450.7 4.1 all-to-all-start.2
  455.0 4.3 copy.23
  459.3 3.7 reshape.167
  463.0 227.6 %all-to-all-done.2 = bf16[32,36,4096]{2,1,0:T(8,128)(2,1)} async-done(((bf16[32,36,4096]{2,1,0:T(8,128)(2,1)}), bf16[32,36,4096]{2,1,0:T(8,128)(2,1)}, u32[]{:S(2)}, u32[]{:S(2)}) %all-to-all-start.2) | async-done | bytes 9437216 | tf_op jit(solution)/shard_map/all_to_all | solution.py:103
  690.6 13.2 %reshape.166 = bf16[1152,4096]{1,0:T(8,128)(2,1)} reshape(bf16[32,36,4096]{2,1,0:T(8,128)(2,1)} %all-to-all-done.2) | data formatting | bytes 18874368 | tf_op jit(solution)/shard_map/reshape | solution.py:104
  703.8 20.0 %gather_fusion.1 = bf16[1024,4096]{1,0:T(8,128)(2,1)} fusion(bf16[1152,4096]{1,0:T(8,128)(2,1)} %reshape.166, s32[1024]{0:T(1024)S(1)} %broadcast_clamp_fusion), kind=kCustom, calls=%fused_computation.1 | custom fusion | bytes 16781312 | tf_op jit(solution)/shard_map/gather | solution.py:105
  723.8 13.2 %fusion = f32[128,4096]{1,0:T(8,128)} fusion(bf16[1024,4096]{1,0:T(8,128)(2,1)} %gather_fusion.1, f32[128,8]{1,0:T(8,128)S(1)} %copy.24), kind=kLoop, calls=%fused_computation.4 | loop fusion | flops 12058624 | bytes 10489856 | tf_op jit(solution)/shard_map/reduce_sum | solution.py:106
  737.0 3.5 fusion.21
  (44 shorter events, 1.6 us)
Async XLA Ops:
  6.5 82.5 %all-gather.2.cloned.1.call-start = ((), (), s32[]{:S(2)}) async-start(), calls=%async_computation.3 | async-start | bytes 5242880 | tf_op jit(solution)/shard_map/all_gather | solution.py:69
  32.7 3.2 copy-start.3
  99.1 19.6 %copy-start.1 = (bf16[1,128,4096]{2,1,0:T(8,128)(2,1)S(1)}, bf16[1,128,4096]{2,1,0:T(8,128)(2,1)}, u32[]{:S(2)}) copy-start(bf16[1,128,4096]{2,1,0:T(8,128)(2,1)} %param.11) | copy-start | bytes 3145732
  99.1 20.0 %copy-start.2 = (f32[4096]{0:T(1024)S(1)}, f32[4096]{0:T(1024)}, u32[]{:S(2)}) copy-start(f32[4096]{0:T(1024)} %param.16) | copy-start | bytes 49156
  99.1 17.7 %all-to-all-start = ((bf16[4,128,1024]{2,1,0:T(8,128)(2,1)}), bf16[4,128,1024]{2,1,0:T(8,128)(2,1)S(1)}, u32[]{:S(2)}, u32[]{:S(2)}) async-start(bf16[4,128,1024]{2,1,0:T(8,128)(2,1)} %bitcast.9), calls=%async_computation | async-start | bytes 2097152 | tf_op jit(solution)/shard_map/all_to_all | solution.py:73
  405.7 12.0 %copy-start = (bf16[1152,4096]{1,0:T(8,128)(2,1)S(1)}, bf16[1152,4096]{1,0:T(8,128)(2,1)}, u32[]{:S(2)}) copy-start(bf16[1152,4096]{1,0:T(8,128)(2,1)} %reshape.164) | copy-start | bytes 28311556
  405.7 22.3 %slice-start = ((s8[6291456]{0:T(1024)(128)(4,1)}), s8[4194304]{0:T(1024)(128)(4,1)S(1)}, s32[]{:S(2)}) async-start(s8[6291456]{0:T(1024)(128)(4,1)} %bitcast.109), calls=%async_computation.4 | async-start | bytes 8388608
  417.7 10.3 %slice-start.1 = ((s8[6291456]{0:T(1024)(128)(4,1)}), s8[2097152]{0:T(1024)(128)(4,1)S(1)}, s32[]{:S(2)}) async-start(s8[6291456]{0:T(1024)(128)(4,1)} %bitcast.109), calls=%async_computation.5 | async-start | bytes 4194304
  450.7 4.1 copy-start.4
  450.7 239.9 %all-to-all-start.2 = ((bf16[32,36,4096]{2,1,0:T(8,128)(2,1)}), bf16[32,36,4096]{2,1,0:T(8,128)(2,1)}, u32[]{:S(2)}, u32[]{:S(2)}) async-start(bf16[32,36,4096]{2,1,0:T(8,128)(2,1)} %reshape.165), calls=%async_computation.2 | async-start | bytes 20971520 | tf_op jit(solution)/shard_map/all_to_all | solution.py:103
Sparse Core Ops, SparseCore 0:
  36.1 52.8 all-gather.1
where the time goes:
time: 756 us; the launch traced here: 748 us
  waiting for transfers between devices  284 us (38%)
  blocking collectives  253 us (33%)
  local copies, waits for them, and re-layouts  111 us (15%)
  matrix products  47.2 us (6%)
  other arithmetic  30.5 us (4%)
  between operations  14.1 us (2%)
  starting transfers between devices  7.91 us (1%)
    all_to_all x1, blocking collectives, local(): lax.all_to_all(outgoing, ('dp', 'ctx'), split_axis=0, concat_axis=0, tile...  234 us
    all_to_all x1, waiting for transfers between devices, local(): lax.all_to_all(served, ('dp', 'ctx'), split_axis=0, concat_axis=0, tiled=...  228 us
    all_gather x1, waiting for transfers between devices, local(): lax.all_gather(attended, 'ctx', axis=0, tiled=True)  43.1 us
    gather x1, local copies, waits for them, and re-layouts, local(): picked = returned[slot_index].reshape(tok_count, TOP, model_width)  20 us
    scatter x1, local copies, waits for them, and re-layouts, local(): outgoing = jnp.zeros((expert_total * capacity, model_width), jnp.bfloat16...  18.4 us
  transfers between devices with their start and end apart: 3, of which 3 were waited for; matrix products, arithmetic and copies ran while one was open for 2% of the time, Pallas kernels for 0%

commit v1 on v0

--- a/solution.py
+++ b/solution.py
@@ -81,18 +81,16 @@
     slot_gates = score_rows / jnp.sum(score_rows, axis=1, keepdims=True)
     expert_total = lax.axis_size(("dp", "ctx"))
     capacity = max(2, tok_count * TOP * 9 // (8 * expert_total))
-    expert_ids = routes[0].reshape(tok_count * TOP)
-    one_hot = (expert_ids[:, None] == jnp.arange(expert_total, dtype=jnp.int32)[None, :]).astype(
-        jnp.int32
-    )
-    earlier = jnp.sum((jnp.cumsum(one_hot, axis=0) - one_hot) * one_hot, axis=1)
-    slot_index = expert_ids * capacity + earlier
-    token_of = jnp.arange(tok_count * TOP, dtype=jnp.int32) // TOP
-    outgoing = (
-        jnp.zeros((expert_total * capacity, model_width), jnp.bfloat16)
-        .at[slot_index]
-        .set(normed[token_of])
-    )
+    named = routes[0][:, :, None] == jnp.arange(expert_total, dtype=jnp.int32)
+    chosen = jnp.any(named, axis=1)
+    gate_of = jnp.sum(jnp.where(named, slot_gates[:, :, None], 0.0), axis=1)
+    row = jnp.arange(tok_count, dtype=jnp.int32)
+    before = (row[None, :] < row[:, None]).astype(jnp.bfloat16)
+    rank = jnp.dot(before, chosen.astype(jnp.bfloat16), preferred_element_type=jnp.float32)
+    rank = jnp.where(chosen, rank.astype(jnp.int32), -1)
+    place = rank.T[:, None, :] == jnp.arange(capacity, dtype=jnp.int32)[None, :, None]
+    pick = place.astype(jnp.bfloat16).reshape(expert_total * capacity, tok_count)
+    outgoing = jnp.dot(pick, normed, preferred_element_type=jnp.float32).astype(jnp.bfloat16)
     outgoing = outgoing.reshape(expert_total, capacity, model_width)
     served = expert_ffn(
         lax.all_to_all(outgoing, ("dp", "ctx"), split_axis=0, concat_axis=0, tiled=True),
@@ -102,8 +100,13 @@
     )
     returned = lax.all_to_all(served, ("dp", "ctx"), split_axis=0, concat_axis=0, tiled=True)
     returned = returned.reshape(expert_total * capacity, model_width)
-    picked = returned[slot_index].reshape(tok_count, TOP, model_width)
-    mixture = jnp.sum(slot_gates[:, :, None] * picked.astype(jnp.float32), axis=1)
+    blend = jnp.where(place, gate_of.T[:, None, :], 0.0).reshape(expert_total * capacity, tok_count)
+    high = blend.astype(jnp.bfloat16)
+    low = (blend - high.astype(jnp.float32)).astype(jnp.bfloat16)
+    over_slots = (((0,), (0,)), ((), ()))
+    mixture = lax.dot_general(
+        high, returned, over_slots, preferred_element_type=jnp.float32
+    ) + lax.dot_general(low, returned, over_slots, preferred_element_type=jnp.float32)
     return (residual + mixture).astype(jnp.bfloat16)[None]
 
 

time: 756 us -> 703 us (0.930)
  local copies, waits for them, and re-layouts: 111 us -> 50 us
  other arithmetic: 30.5 us -> 5.77 us
  matrix products: 47.2 us -> 69.5 us
  waiting for transfers between devices: 284 us -> 302 us
    gather x2 -> x0, local copies, waits for them, and re-layouts: 27.7 us -> none  [the longest x1 20 us: local(): picked = returned[slot_index].reshape(tok_count, TOP, model_width)]
    dot_general x0 -> x4, matrix products: none -> 19.2 us  [the longest x1 6.84 us: local(): lax.dot_general(high, returned, over_slots, preferred_element_type=jnp.fl...]
    scatter x1 -> x0, local copies, waits for them, and re-layouts: 18.4 us -> none  [local(): outgoing = jnp.zeros((expert_total * capacity, model_width), jnp.bfloat16...]
    reduce_sum x2 -> x1, other arithmetic: 13.3 us -> 0.02 us  [local(): gate_of = jnp.sum(jnp.where(named, slot_gates[:, :, None], 0.0), axis=1)]
    reshape x1 -> x0, local copies, waits for them, and re-layouts: 13.2 us -> none  [local(): returned = returned.reshape(expert_total * capacity, model_width)]
    all_gather x1, waiting for transfers between devices: 43.1 us -> 53 us  [local(): lax.all_gather(attended, 'ctx', axis=0, tiled=True)]
    another operation x3 -> x0, other arithmetic: 9.14 us -> none
    all_to_all x1, waiting for transfers between devices: 228 us -> 235 us  [local(): lax.all_to_all(served, ('dp', 'ctx'), split_axis=0, concat_axis=0, tiled=...]
  transfers between devices with their start and end apart: 3 -> 3, of which waited for: 3 -> 3; matrix products, arithmetic and copies ran while one was open for 2% -> 0% of each run, Pallas kernels for 0% -> 0%
where the time goes in v1:
time: 703 us; the launch traced here: 701 us
  waiting for transfers between devices  302 us (43%)
  blocking collectives  253 us (36%)
  matrix products  69.5 us (10%)
  local copies, waits for them, and re-layouts  50 us (7%)
  between operations  13.6 us (2%)
  starting transfers between devices  7.72 us (1%)
    all_to_all x1, waiting for transfers between devices, local(): lax.all_to_all(served, ('dp', 'ctx'), split_axis=0, concat_axis=0, tiled=...  235 us
    all_to_all x1, blocking collectives, local(): lax.all_to_all(outgoing, ('dp', 'ctx'), split_axis=0, concat_axis=0, tile...  234 us
    all_gather x1, waiting for transfers between devices, local(): lax.all_gather(attended, 'ctx', axis=0, tiled=True)  53 us
  transfers between devices with their start and end apart: 3, of which 3 were waited for; matrix products, arithmetic and copies ran while one was open for 0% of the time, Pallas kernels for 0%

profile of v1, /device:TPU:0, one launch (start us, length us, event | category | flops | bytes accessed | tf_op | source)
XLA Modules:
  0.0 701.3 jit_solution(12589547528910131386)
XLA Ops:
  6.6 1.4 copy.41
  8.1 1.0 copy.28
  9.0 10.4 %all_gather.9 = bf16[1,512,256]{1,2,0:T(8,128)(2,1)S(1)} all-gather(bf16[1,128,256]{1,2,0:T(8,128)(2,1)S(1)} %copy.28), channel_id=1, replica_groups=mesh['dp'=8,'ctx'=4] {'ctx'}, dimensions={1}, use_global_device_ids=true | all-gather | bytes 327680 | tf_op jit(solution)/shard_map/all_gather | solution.py:41
  19.5 5.2 fusion
  24.7 9.0 %all_gather.10 = bf16[1,512,256]{2,1,0:T(8,128)(2,1)S(1)} all-gather(bf16[1,128,256]{2,1,0:T(8,128)(2,1)S(1)} %copy-done.3), channel_id=1, replica_groups=mesh['dp'=8,'ctx'=4] {'ctx'}, dimensions={1}, use_global_device_ids=true | all-gather | bytes 327680 | tf_op jit(solution)/shard_map/all_gather | solution.py:42
  33.6 0.1 copy.31
  33.8 4.6 fusion.6
  38.5 1.2 copy-done
  39.6 3.2 fusion.25
  42.9 53.0 %all-gather.2.cloned.1.call-done = bf16[512,4096]{0,1:T(8,128)(2,1)} async-done(((bf16[128,4096]{0,1:T(8,128)(2,1)}), bf16[512,4096]{0,1:T(8,128)(2,1)}) %all-gather.2.cloned.1.call-update) | async-done | bytes 4194320 | tf_op jit(solution)/shard_map/all_gather | solution.py:69
  95.8 10.1 %convolution_convert_fusion.2 = bf16[512,1024]{1,0:T(8,128)(2,1)} fusion(bf16[512,4096]{0,1:T(8,128)(2,1)} %all-gather.2.cloned.1.call-done, bf16[4096,1024]{1,0:T(8,128)(2,1)} %param.15), kind=kOutput, calls=%fused_computation.33 | convolution fusion | flops 4295491584 | bytes 13631488 | tf_op jit(solution)/shard_map/dot_general | solution.py:68
  106.0 3.8 all-to-all-start
  109.8 0.1 fusion.28
  110.0 0.1 iota_compare_fusion
  110.2 13.3 %all-to-all-done = bf16[4,128,1024]{2,1,0:T(8,128)(2,1)S(1)} async-done(((bf16[4,128,1024]{2,1,0:T(8,128)(2,1)}), bf16[4,128,1024]{2,1,0:T(8,128)(2,1)S(1)}, u32[]{:S(2)}, u32[]{:S(2)}) %all-to-all-start) | async-done | bytes 1048608 | tf_op jit(solution)/shard_map/all_to_all | solution.py:73
  123.5 0.5 convert_bitcast_fusion
  124.0 0.1 copy.40
  124.2 0.4 multiply_reduce_fusion
  124.6 2.7 copy.33
  127.3 3.7 reshape.139
  130.9 6.7 convolution_convert_fusion.1
  137.6 13.2 %reshape.134 = bf16[32,36,4096]{2,1,0:T(8,128)(2,1)} reshape(bf16[1152,4096]{1,0:T(8,128)(2,1)} %convolution_convert_fusion.1) | data formatting | bytes 18874368 | tf_op jit(solution)/shard_map/reshape | solution.py:94
  150.8 233.5 %all_to_all.23 = bf16[32,36,4096]{2,1,0:T(8,128)(2,1)} all-to-all(bf16[32,36,4096]{2,1,0:T(8,128)(2,1)} %reshape.134), channel_id=1, replica_groups=mesh['dp'=8,'ctx'=4] {'dp','ctx'}, dimensions={0} | all-to-all | bytes 18874368 | tf_op jit(solution)/shard_map/all_to_all | solution.py:96
  384.4 13.3 %reshape.135 = bf16[1152,4096]{1,0:T(8,128)(2,1)} reshape(bf16[32,36,4096]{2,1,0:T(8,128)(2,1)} %all_to_all.23) | data formatting | bytes 18874368 | tf_op jit(solution)/shard_map/reshape | solution.py:13
  397.7 12.0 %fusion.4 = f32[1152,768]{1,0:T(8,128)S(1)} fusion(bf16[1152,4096]{1,0:T(8,128)(2,1)} %reshape.135, bf16[1,4096,768]{2,1,0:T(8,128)(2,1)} %param.19), kind=kOutput, calls=%fused_computation.8 | convolution fusion | flops 7247757312 | bytes 19267584 | tf_op jit(solution)/shard_map/dot_general | solution.py:14
  409.7 10.3 %fusion.18 = bf16[1152,768]{1,0:T(8,128)(2,1)S(1)} fusion(bf16[1152,4096]{1,0:T(8,128)(2,1)S(1)} %copy-done.2, bf16[1,4096,768]{2,1,0:T(8,128)(2,1)} %param.20, f32[1152,768]{1,0:T(8,128)S(1)} %fusion.4), kind=kOutput, calls=%fused_computation.21 | convolution fusion | flops 7253065728 | bytes 21037056 | tf_op jit(solution)/shard_map/dot_general | solution.py:15
  420.0 9.5 %convolution_convert_fusion = bf16[1152,4096]{1,0:T(8,128)(2,1)} fusion(bf16[1152,768]{1,0:T(8,128)(2,1)S(1)} %fusion.18, bf16[1,768,4096]{2,1,0:T(8,128)(2,1)S(1)} %bitcast.107), kind=kOutput, calls=%fused_computation | convolution fusion | flops 7252475904 | bytes 17498112 | tf_op jit(solution)/shard_map/dot_general | solution.py:17
  429.5 13.2 %reshape.136 = bf16[32,36,4096]{2,1,0:T(8,128)(2,1)} reshape(bf16[1152,4096]{1,0:T(8,128)(2,1)} %convolution_convert_fusion) | data formatting | bytes 18874368 | tf_op jit(solution)/shard_map/reshape | solution.py:18
  442.7 3.9 all-to-all-start.2
  446.6 235.5 %all-to-all-done.2 = bf16[32,36,4096]{2,1,0:T(8,128)(2,1)} async-done(((bf16[32,36,4096]{2,1,0:T(8,128)(2,1)}), bf16[32,36,4096]{2,1,0:T(8,128)(2,1)}, u32[]{:S(2)}, u32[]{:S(2)}) %all-to-all-start.2) | async-done | bytes 9437216 | tf_op jit(solution)/shard_map/all_to_all | solution.py:101
  682.1 5.5 convolution_bitcast_fusion
  687.6 6.8 fusion.11
  (29 shorter events, 0.3 us)
Async XLA Ops:
  6.5 18.2 %copy-start.3 = (bf16[1,128,256]{2,1,0:T(8,128)(2,1)S(1)}, bf16[1,128,256]{2,1,0:T(8,128)(2,1)}, u32[]{:S(2)}) copy-start(bf16[1,128,256]{2,1,0:T(8,128)(2,1)} %param.14) | copy-start | bytes 196612
  6.5 89.3 %all-gather.2.cloned.1.call-start = ((), (), s32[]{:S(2)}) async-start(), calls=%async_computation.3 | async-start | bytes 5242880 | tf_op jit(solution)/shard_map/all_gather | solution.py:69
  33.8 5.8 copy-start
  42.8 67.0 %copy-start.6 = (s32[1,128,8]{1,2,0:T(8,128)S(1)}, s32[1,128,8]{1,2,0:T(8,128)}, u32[]{:S(2)}) copy-start(s32[1,128,8]{1,2,0:T(8,128)} %param.17) | copy-start | bytes 12292
  106.0 18.2 %copy-start.1 = (bf16[1,128,4096]{2,1,0:T(8,128)(2,1)S(1)}, bf16[1,128,4096]{2,1,0:T(8,128)(2,1)}, u32[]{:S(2)}) copy-start(bf16[1,128,4096]{2,1,0:T(8,128)(2,1)} %param.11) | copy-start | bytes 3145732
  106.0 17.5 %all-to-all-start = ((bf16[4,128,1024]{2,1,0:T(8,128)(2,1)}), bf16[4,128,1024]{2,1,0:T(8,128)(2,1)S(1)}, u32[]{:S(2)}, u32[]{:S(2)}) async-start(bf16[4,128,1024]{2,1,0:T(8,128)(2,1)} %bitcast.10), calls=%async_computation | async-start | bytes 2097152 | tf_op jit(solution)/shard_map/all_to_all | solution.py:73
  124.2 6.8 copy-start.4
  397.6 12.0 %copy-start.2 = (bf16[1152,4096]{1,0:T(8,128)(2,1)S(1)}, bf16[1152,4096]{1,0:T(8,128)(2,1)}, u32[]{:S(2)}) copy-start(bf16[1152,4096]{1,0:T(8,128)(2,1)} %reshape.135) | copy-start | bytes 28311556
  397.7 22.3 %slice-start = ((s8[6291456]{0:T(1024)(128)(4,1)}), s8[4194304]{0:T(1024)(128)(4,1)S(1)}, s32[]{:S(2)}) async-start(s8[6291456]{0:T(1024)(128)(4,1)} %bitcast.106), calls=%async_computation.4 | async-start | bytes 8388608
  409.7 10.3 %slice-start.1 = ((s8[6291456]{0:T(1024)(128)(4,1)}), s8[2097152]{0:T(1024)(128)(4,1)S(1)}, s32[]{:S(2)}) async-start(s8[6291456]{0:T(1024)(128)(4,1)} %bitcast.106), calls=%async_computation.5 | async-start | bytes 4194304
  442.7 3.9 copy-start.5
  442.7 239.4 %all-to-all-start.2 = ((bf16[32,36,4096]{2,1,0:T(8,128)(2,1)}), bf16[32,36,4096]{2,1,0:T(8,128)(2,1)}, u32[]{:S(2)}, u32[]{:S(2)}) async-start(bf16[32,36,4096]{2,1,0:T(8,128)(2,1)} %reshape.136), calls=%async_computation.2 | async-start | bytes 20971520 | tf_op jit(solution)/shard_map/all_to_all | solution.py:101
Sparse Core Ops, SparseCore 0:
  43.0 52.8 all-gather.1

commit v2 on v0

--- a/solution.py
+++ b/solution.py
@@ -1,21 +1,317 @@
+import functools
+
 import jax
 import jax.numpy as jnp
 from jax import lax
+from jax.experimental import pallas as pl
+from jax.experimental.pallas import tpu as pltpu
 from jax.sharding import PartitionSpec as P
 
 HQ = 32
 KVH = 2
 DH = 128
 TOP = 8
-
-
-def expert_ffn(slots_in, w_gate, w_up, w_down):
-    flat_rows = slots_in.reshape(-1, slots_in.shape[-1])
-    gated = jnp.dot(flat_rows, w_gate, preferred_element_type=jnp.float32)
-    lifted = jnp.dot(flat_rows, w_up, preferred_element_type=jnp.float32)
-    activated = (jax.nn.silu(gated) * lifted).astype(jnp.bfloat16)
-    result = jnp.dot(activated, w_down, preferred_element_type=jnp.float32).astype(jnp.bfloat16)
-    return result.reshape(slots_in.shape)
+MESH = pl.DeviceIdType.MESH
+
+
+def _ceil(count, unit):
+    return -(-count // unit) * unit
+
+
+def _tiles(rows, cols, mt, nt, body):
+    def step(i, carry):
+        m, n = i // (cols // nt), i % (cols // nt)
+        body(pl.ds(pl.multiple_of(m * mt, mt), mt), pl.ds(pl.multiple_of(n * nt, nt), nt))
+        return carry
+
+    lax.fori_loop(0, (rows // mt) * (cols // nt), step, 0)
+
+
+def _moe_kernel(
+    dims,
+    normed,
+    residual,
+    pick,
+    spread,
+    gate_rows,
+    w_gate,
+    w_up,
+    w_down,
+    out,
+    tokens,
+    sent,
+    got,
+    gated,
+    lifted,
+    act,
+    partials,
+    wgu,
+    wd,
+    z_send,
+    z_recv,
+    x_send,
+    x_recv,
+    p_send,
+    p_recv,
+    w_sem,
+    d_sem,
+    credit,
+):
+    planes, ctx_n, chunks, tok, slots = dims
+    peers = 2 * ctx_n
+    rows = peers * slots
+    dc = normed.shape[1] // chunks
+    hid = gated.shape[1]
+    mt = rows // 4
+    nt = min(256, dc)
+    dp, cx = lax.axis_index("dp"), lax.axis_index("ctx")
+    z, core = dp // 2, dp % 2
+    me = core * ctx_n + cx
+
+    def in_plane(j):
+        j = lax.rem(j + peers, peers)
+        return (2 * z + j // ctx_n, lax.rem(j, ctx_n))
+
+    def along(q):
+        return (2 * lax.rem(q + planes, planes) + core, cx)
+
+    def dot(a, b):
+        return jnp.dot(a, b, preferred_element_type=jnp.float32)
+
+    def load_gu(c):
+        return [
+            pltpu.make_async_copy(
+                w.at[0, pl.ds(c * dc, dc), :], wgu.at[c % 2, i], w_sem.at[c % 2, i]
+            )
+            for i, w in enumerate((w_gate, w_up))
+        ]
+
+    def load_down(c):
+        return pltpu.make_async_copy(
+            w_down.at[0, :, pl.ds(c * dc, dc)], wd.at[c % 2], d_sem.at[c % 2]
+        )
+
+    def z_copy(c, q):
+        return pltpu.make_async_remote_copy(
+            src_ref=tokens.at[c, pl.ds(0, tok)],
+            dst_ref=tokens.at[c, pl.ds(q * tok, tok)],
+            send_sem=z_send.at[c, q - 1],
+            recv_sem=z_recv.at[c, q - 1],
+            device_id=along(z + q),
+            device_id_type=MESH,
+        )
+
+    def x_copy(c, k, back):
+        return pltpu.make_async_remote_copy(
+            src_ref=sent.at[c, pl.ds(k * slots, slots)],
+            dst_ref=got.at[c, pl.ds(k * slots, slots)],
+            send_sem=x_send.at[c, k - 1],
+            recv_sem=x_recv.at[c, k - 1],
+            device_id=in_plane(me - k if back else me + k),
+            device_id_type=MESH,
+        )
+
+    def p_copy(c, q):
+        return pltpu.make_async_remote_copy(
+            src_ref=tokens.at[c, pl.ds(q * tok, tok)],
+            dst_ref=partials.at[c, pl.ds((q - 1) * tok, tok)],
+            send_sem=p_send.at[c, q - 1],
+            recv_sem=p_recv.at[c, q - 1],
+            device_id=along(z - q),
+            device_id_type=MESH,
+        )
+
+    for c in range(min(2, chunks)):
+        for copy in load_gu(c):
+            copy.start()
+        load_down(c).start()
+    for c in range(chunks):
+        tokens[c, pl.ds(0, tok), :] = normed[:, pl.ds(c * dc, dc)]
+    barrier = pltpu.get_barrier_semaphore()
+    for q in range(1, planes):
+        pl.semaphore_signal(barrier, inc=1, device_id=along(z + q), device_id_type=MESH)
+    for k in range(1, peers):
+        pl.semaphore_signal(barrier, inc=1, device_id=in_plane(me + k), device_id_type=MESH)
+    pl.semaphore_wait(barrier, planes - 1 + peers - 1)
+    for c in range(chunks):
+        for q in range(1, planes):
+            z_copy(c, q).start()
+
+    def enter(c):
+        for k in range(1, peers):
+            x_copy(c, k, False).wait_recv()
+        for copy in load_gu(c):
+            copy.wait()
+
+        def body(m, n):
+            x = got[c, m, :]
+            g = dot(x, wgu[c % 2, 0, :, n])
+            u = dot(x, wgu[c % 2, 1, :, n])
+            if c == 0:
+                gated[m, n] = g
+                lifted[m, n] = u
+            elif c < chunks - 1:
+                gated[m, n] += g
+                lifted[m, n] += u
+            else:
+                g = g + gated[m, n]
+                u = u + lifted[m, n]
+                act[m, n] = (g / (1.0 + jnp.exp(-g)) * u).astype(jnp.bfloat16)
+
+        _tiles(rows, hid, mt, min(256, hid), body)
+        if c + 2 < chunks:
+            for copy in load_gu(c + 2):
+                copy.start()
+
+    for c in range(chunks):
+        for q in range(1, planes):
+            z_copy(c, q).wait_recv()
+
+        def body(m, n, c=c):
+            sent[c, m, n] = dot(pick[m, :], tokens[c, :, n]).astype(jnp.bfloat16)
+
+        _tiles(rows, dc, mt, nt, body)
+        for k in range(1, peers):
+            x_copy(c, k, False).start()
+        got[c, pl.ds(0, slots), :] = sent[c, pl.ds(0, slots), :]
+        if c > 0:
+            enter(c - 1)
+    enter(chunks - 1)
+    for k in range(1, peers):
+        pl.semaphore_signal(credit, inc=1, device_id=in_plane(me + k), device_id_type=MESH)
+
+    def leave(c):
+        for k in range(1, peers):
+            x_copy(c, k, True).wait_recv()
+        for q in range(1, planes):
+            z_copy(c, q).wait_send()
+
+        def body(m, n):
+            tokens[c, m, n] = dot(spread[m, :], got[c, :, n]).astype(jnp.bfloat16)
+
+        _tiles(planes * tok, dc, tok, nt, body)
+        for q in range(1, planes):
+            p_copy(c, q).start()
+
+    for c in range(chunks):
+        for k in range(1, peers):
+            x_copy(c, k, False).wait_send()
+        load_down(c).wait()
+
+        def body(m, n, c=c):
+            y = dot(act[m, :], wd[c % 2, :, n]) * gate_rows[m, :]
+            sent[c, m, n] = y.astype(jnp.bfloat16)
+
+        _tiles(rows, dc, mt, nt, body)
+        if c + 2 < chunks:
+            load_down(c + 2).start()
+        if c == 0:
+            pl.semaphore_wait(credit, peers - 1)
+        for k in range(1, peers):
+            x_copy(c, k, True).start()
+        got[c, pl.ds(0, slots), :] = sent[c, pl.ds(0, slots), :]
+        if c > 0:
+            leave(c - 1)
+    leave(chunks - 1)
+    for c in range(chunks):
+        for q in range(1, planes):
+            p_copy(c, q).wait_recv()
+        total = residual[:, pl.ds(c * dc, dc)] + tokens[c, pl.ds(0, tok), :].astype(jnp.float32)
+        for q in range(1, planes):
+            total += partials[c, pl.ds((q - 1) * tok, tok), :].astype(jnp.float32)
+        out[:, pl.ds(c * dc, dc)] = total.astype(jnp.bfloat16)
+    for c in range(chunks):
+        for k in range(1, peers):
+            x_copy(c, k, True).wait_send()
+        for q in range(1, planes):
+            p_copy(c, q).wait_send()
+
+
+def moe(planes, ctx_n, slots, normed, residual, pick, spread, gate_rows, w_gate, w_up, w_down):
+    tok, width = normed.shape
+    hid = w_gate.shape[2]
+    chunks = max(4, planes)
+    peers = 2 * ctx_n
+    rows = peers * slots
+    dc = width // chunks
+    dims = (planes, ctx_n, chunks, tok, slots)
+    vmem = pl.BlockSpec(memory_space=pltpu.VMEM)
+    hbm = pl.BlockSpec(memory_space=pl.ANY)
+    dma = pltpu.SemaphoreType.DMA
+    return pl.pallas_call(
+        functools.partial(_moe_kernel, dims),
+        out_shape=jax.ShapeDtypeStruct((tok, width), jnp.bfloat16),
+        in_specs=[vmem] * 5 + [hbm] * 3,
+        out_specs=vmem,
+        scratch_shapes=[
+            pltpu.VMEM((chunks, planes * tok, dc), jnp.bfloat16),
+            pltpu.VMEM((chunks, rows, dc), jnp.bfloat16),
+            pltpu.VMEM((chunks, rows, dc), jnp.bfloat16),
+            pltpu.VMEM((rows, hid), jnp.float32),
+            pltpu.VMEM((rows, hid), jnp.float32),
+            pltpu.VMEM((rows, hid), jnp.bfloat16),
+            pltpu.VMEM((chunks, (planes - 1) * tok, dc), jnp.bfloat16),
+            pltpu.VMEM((2, 2, dc, hid), jnp.bfloat16),
+            pltpu.VMEM((2, hid, dc), jnp.bfloat16),
+            dma((chunks, planes - 1)),
+            dma((chunks, planes - 1)),
+            dma((chunks, peers - 1)),
+            dma((chunks, peers - 1)),
+            dma((chunks, planes - 1)),
+            dma((chunks, planes - 1)),
+            dma((2, 2)),
+            dma((2,)),
+            pltpu.SemaphoreType.REGULAR,
+        ],
+        compiler_params=pltpu.CompilerParams(
+            collective_id=0, has_side_effects=True, vmem_limit_bytes=62 * 1024 * 1024
+        ),
+        cost_estimate=pl.CostEstimate(
+            flops=6 * rows * width * hid, bytes_accessed=6 * width * hid, transcendentals=rows * hid
+        ),
+    )(normed, residual, pick, spread, gate_rows, w_gate, w_up, w_down)
+
+
+def slot_places(named, before, capacity):
+    rank = jnp.einsum(
+        "kqs,st->kqt", named.astype(jnp.bfloat16), before, preferred_element_type=jnp.float32
+    ).astype(jnp.int32)
+    first = (jnp.arange(named.shape[1], dtype=jnp.int32) * capacity)[None, :, None]
+    return jnp.where(named, rank + first, -1).reshape(named.shape[0], -1)
+
+
+def countdown(blocks, start):
+    count = blocks.shape[0]
+    back = jnp.flip(blocks, 0)
+    return lax.dynamic_slice_in_dim(jnp.concatenate([back, back]), count - 1 - start, count)
+
+
+def tables(routes, slot_gates, capacity):
+    tok = routes.shape[0]
+    dp_n, ctx_n = lax.axis_size("dp"), lax.axis_size("ctx")
+    planes, peers = dp_n // 2, 2 * ctx_n
+    slots = _ceil(planes * capacity, 16)
+    dp, cx = lax.axis_index("dp"), lax.axis_index("ctx")
+    z, me = dp // 2, (dp % 2) * ctx_n + cx
+    ids = lax.all_gather(routes.T, ("dp", "ctx"), axis=0).reshape(planes, peers, TOP, tok)
+    gates = lax.all_gather(slot_gates.T, ("dp", "ctx"), axis=0).reshape(planes, peers, TOP, tok)
+    k = jnp.arange(peers, dtype=jnp.int32)
+    row = jnp.arange(tok, dtype=jnp.int32)
+    before = (row[:, None] < row[None, :]).astype(jnp.bfloat16)
+    slot = jnp.arange(slots, dtype=jnp.int32)[None, :, None]
+    ids, gates = countdown(ids, z), countdown(gates, z)
+    mine = lax.dynamic_index_in_dim(ids, me, 1, keepdims=False)
+    target = z * peers + (me + k) % peers
+    named = jnp.any(mine[None] == target[:, None, None, None], axis=2)
+    pick = slot_places(named, before, capacity)[:, None, :] == slot
+    pick = pick.astype(jnp.bfloat16).reshape(peers * slots, planes * tok)
+    hit = ids == z * peers + me
+    named = countdown(jnp.any(hit, axis=2).transpose(1, 0, 2), me)
+    gate = countdown(jnp.sum(jnp.where(hit, gates, 0.0), axis=2).transpose(1, 0, 2), me)
+    arrives = slot_places(named, before, capacity)[:, None, :] == slot
+    gate = gate.reshape(peers, 1, planes * tok)
+    gate_rows = jnp.sum(jnp.where(arrives, gate, 0.0), axis=2).reshape(peers * slots, 1)
+    return planes, ctx_n, slots, pick, pick.T, gate_rows
 
 
 def local(
@@ -81,30 +377,20 @@
     slot_gates = score_rows / jnp.sum(score_rows, axis=1, keepdims=True)
     expert_total = lax.axis_size(("dp", "ctx"))
     capacity = max(2, tok_count * TOP * 9 // (8 * expert_total))
-    expert_ids = routes[0].reshape(tok_count * TOP)
-    one_hot = (expert_ids[:, None] == jnp.arange(expert_total, dtype=jnp.int32)[None, :]).astype(
-        jnp.int32
-    )
-    earlier = jnp.sum((jnp.cumsum(one_hot, axis=0) - one_hot) * one_hot, axis=1)
-    slot_index = expert_ids * capacity + earlier
-    token_of = jnp.arange(tok_count * TOP, dtype=jnp.int32) // TOP
-    outgoing = (
-        jnp.zeros((expert_total * capacity, model_width), jnp.bfloat16)
-        .at[slot_index]
-        .set(normed[token_of])
-    )
-    outgoing = outgoing.reshape(expert_total, capacity, model_width)
-    served = expert_ffn(
-        lax.all_to_all(outgoing, ("dp", "ctx"), split_axis=0, concat_axis=0, tiled=True),
-        gate_weight[0],
-        up_weight[0],
-        down_weight[0],
-    )
-    returned = lax.all_to_all(served, ("dp", "ctx"), split_axis=0, concat_axis=0, tiled=True)
-    returned = returned.reshape(expert_total * capacity, model_width)
-    picked = returned[slot_index].reshape(tok_count, TOP, model_width)
-    mixture = jnp.sum(slot_gates[:, :, None] * picked.astype(jnp.float32), axis=1)
-    return (residual + mixture).astype(jnp.bfloat16)[None]
+    planes, ctx_n, slots, pick, spread, gate_rows = tables(routes[0], slot_gates, capacity)
+    return moe(
+        planes,
+        ctx_n,
+        slots,
+        normed,
+        residual,
+        pick,
+        spread,
+        gate_rows,
+        gate_weight,
+        up_weight,
+        down_weight,
+    )[None]
 
 
 def solution(mesh):

time: 756 us -> 492 us (0.65)
  waiting for transfers between devices: 284 us -> 3.05 us
  Pallas kernels: 0 us -> 279 us
  blocking collectives: 253 us -> 151 us
  local copies, waits for them, and re-layouts: 111 us -> 13.4 us
  matrix products: 47.2 us -> 16.2 us
  other arithmetic: 30.5 us -> 9.55 us
    pallas_call x0 -> x1, Pallas kernels: none -> 279 us  [moe(): pl.pallas_call(functools.partial(_moe_kernel, dims), out_shape=jax.ShapeD...]
    all_to_all x1 -> x0, blocking collectives: 234 us -> none  [local(): lax.all_to_all(outgoing, ('dp', 'ctx'), split_axis=0, concat_axis=0, tile...]
    all_to_all x1 -> x0, waiting for transfers between devices: 228 us -> none  [local(): lax.all_to_all(served, ('dp', 'ctx'), split_axis=0, concat_axis=0, tiled=...]
    all_gather x0 -> x2, blocking collectives: none -> 131 us  [the longest x1 65.7 us: tables(): lax.all_gather(routes.T, ('dp', 'ctx'), axis=0)]
    reshape x4 -> x1, local copies, waits for them, and re-layouts: 52.8 us -> 1.09 us  [tables(): jnp.sum(jnp.where(arrives, gate, 0.0), axis=2).reshape(peers * slots, 1)]
    all_gather x1, waiting for transfers between devices: 43.1 us -> 0.02 us  [local(): lax.all_gather(attended, 'ctx', axis=0, tiled=True)]
    dot_general x3 -> x2, matrix products: 31.8 us -> 0.83 us  [slot_places(): jnp.einsum('kqs,st->kqt', named.astype(jnp.bfloat16), before, preferred_e...]
    gather x2 -> x0, local copies, waits for them, and re-layouts: 27.7 us -> none  [the longest x1 20 us: local(): picked = returned[slot_index].reshape(tok_count, TOP, model_width)]
  transfers between devices with their start and end apart: 3 -> 2, of which waited for: 3 -> 1; matrix products, arithmetic and copies ran while one was open for 2% -> 2% of each run, Pallas kernels for 0% -> 0%
where the time goes in v2:
time: 492 us; the launch traced here: 490 us
  Pallas kernels  279 us (57%)
  blocking collectives  151 us (31%)
  matrix products  16.2 us (3%)
  between operations  13.7 us (3%)
  local copies, waits for them, and re-layouts  13.4 us (3%)
  other arithmetic  9.55 us (2%)
    pallas_call x1, Pallas kernels, moe(): pl.pallas_call(functools.partial(_moe_kernel, dims), out_shape=jax.ShapeD...  279 us
    all_gather x1, blocking collectives, tables(): lax.all_gather(routes.T, ('dp', 'ctx'), axis=0)  65.7 us
    all_gather x1, blocking collectives, tables(): lax.all_gather(slot_gates.T, ('dp', 'ctx'), axis=0)  65.6 us
    all_gather x1, blocking collectives, local(): value_piece = lax.all_gather(values, 'ctx', axis=1, tiled=True)  10.7 us
    dot_general x1, matrix products, local(): jnp.dot(lax.all_gather(attended, 'ctx', axis=0, tiled=True), out_weight,...  10.1 us
  transfers between devices with their start and end apart: 2, of which 1 were waited for; matrix products, arithmetic and copies ran while one was open for 2% of the time, Pallas kernels for 0%

profile of v2, /device:TPU:0, one launch (start us, length us, event | category | flops | bytes accessed | tf_op | source)
XLA Modules:
  0.0 490.0 jit_solution(14335101414615218698)
XLA Ops:
  6.5 10.7 %all_gather.22 = bf16[1,512,256]{2,1,0:T(8,128)(2,1)S(1)} all-gather(bf16[1,128,256]{2,1,0:T(8,128)(2,1)} %param.14), channel_id=1, replica_groups=mesh['dp'=8,'ctx'=4] {'ctx'}, dimensions={1}, use_global_device_ids=true | all-gather | bytes 327680 | tf_op jit(solution)/shard_map/all_gather | solution.py:338
  17.2 0.1 copy.38
  17.5 1.0 copy.35
  18.4 8.7 %all_gather.21 = bf16[1,512,256]{1,2,0:T(8,128)(2,1)S(1)} all-gather(bf16[1,128,256]{1,2,0:T(8,128)(2,1)S(1)} %copy.35), channel_id=1, replica_groups=mesh['dp'=8,'ctx'=4] {'ctx'}, dimensions={1}, use_global_device_ids=true | all-gather | bytes 327680 | tf_op jit(solution)/shard_map/all_gather | solution.py:337
  27.1 1.5 copy.52
  28.6 2.1 fusion
  30.7 2.1 fusion.1
  32.7 3.2 fusion.6
  36.0 65.7 %all-gather = s32[256,128]{1,0:T(8,128)S(1)} all-gather(s32[8,128]{1,0:T(8,128)S(1)} %bitcast.89), channel_id=2, replica_groups=mesh['dp'=8,'ctx'=4] {'dp','ctx'}, dimensions={0}, use_global_device_ids=true | all-gather | bytes 135168 | tf_op jit(solution)/shard_map/all_gather | solution.py:296
  101.8 0.1 compare_reduce_fusion
  102.0 0.1 fusion.14
  102.1 1.8 eq.67
  103.8 2.0 copy.43
  106.0 65.6 %all-gather.1 = f32[256,128]{1,0:T(8,128)S(1)} all-gather(f32[8,128]{1,0:T(8,128)S(1)} %fusion.32), channel_id=3, replica_groups=mesh['dp'=8,'ctx'=4] {'dp','ctx'}, dimensions={0}, use_global_device_ids=true | all-gather | bytes 135168 | tf_op jit(solution)/shard_map/all_gather | solution.py:297
  171.8 0.6 rev.19
  172.4 0.7 fusion.11
  173.1 0.2 compare_convert_fusion
  173.4 10.1 %convolution_convert_fusion = bf16[512,1024]{1,0:T(8,128)(2,1)} fusion(bf16[512,4096]{0,1:T(8,128)(2,1)} %all-gather.4.cloned.1.call-done, bf16[4096,1024]{1,0:T(8,128)(2,1)} %param.15), kind=kOutput, calls=%fused_computation.16 | convolution fusion | flops 4295491584 | bytes 13631488 | tf_op jit(solution)/shard_map/dot_general | solution.py:364
  183.5 4.4 all-to-all-start
  187.9 1.4 fusion.26
  189.3 1.5 copy.44.pick
  190.8 1.1 select_reduce_fusion
  191.9 1.1 reshape.77.gate_rows
  193.0 1.2 fusion.46.spread
  194.2 3.0 all-to-all-done
  197.2 1.5 convert_bitcast_fusion
  198.7 0.1 copy.51
  198.9 0.4 multiply_reduce_fusion
  199.3 1.3 copy-done
  200.7 1.2 multiply_convert_fusion.normed
  201.9 279.0 %shard_map.109 = bf16[128,4096]{1,0:T(8,128)(2,1)} custom-call(bf16[128,4096]{1,0:T(8,128)(2,1)} %multiply_convert_fusion.normed, f32[128,4096]{1,0:T(8,128)} %copy-done, bf16[1152,512]{1,0:T(8,128)(2,1)} %copy.44.pick, bf16[512,1152]{1,0:T(8,128)(2,1)} %fusion.46.spread, f32[1152,1]{1,0:T(8,128)} %reshape.77.gate_rows, bf16[1,4096,768]{2,1,0:T(8,128)(2,1)} %w_gate.1, ...), custom_call_target="tpu_custom_call" | custom-call | flops 21743271936 | bytes 18874368 | tf_op jit(solution)/shard_map/pallas_call | solution.py:241
  480.9 2.3 copy.60
  (28 shorter events, 0.5 us)
Async XLA Ops:
  6.5 166.8 %all-gather.4.cloned.1.call-start = ((), (), s32[]{:S(2)}) async-start(), calls=%async_computation.1 | async-start | bytes 5242880 | tf_op jit(solution)/shard_map/all_gather | solution.py:365
  32.7 3.3 copy-start.4
  35.9 70.0 %copy-start.3 = (f32[1,128,8]{1,2,0:T(8,128)S(1)}, f32[1,128,8]{1,2,0:T(8,128)}, u32[]{:S(2)}) copy-start(f32[1,128,8]{1,2,0:T(8,128)} %param.18) | copy-start | bytes 12292
  183.5 13.7 %all-to-all-start = ((bf16[4,128,1024]{2,1,0:T(8,128)(2,1)}), bf16[4,128,1024]{2,1,0:T(8,128)(2,1)}, u32[]{:S(2)}, u32[]{:S(2)}) async-start(bf16[4,128,1024]{2,1,0:T(8,128)(2,1)} %bitcast.81), calls=%async_computation | async-start | bytes 2097152 | tf_op jit(solution)/shard_map/all_to_all | solution.py:369
  194.2 4.7 copy-start.1
  198.7 2.0 copy-start.2
  199.3 1.4 copy-start
Sparse Core Ops, SparseCore 0:
  36.1 54.0 all-gather.3

commit v3 on v2

--- a/solution.py
+++ b/solution.py
@@ -11,6 +11,7 @@
 KVH = 2
 DH = 128
 TOP = 8
+AHEAD = 2
 MESH = pl.DeviceIdType.MESH
 
 
@@ -33,7 +34,6 @@
     residual,
     pick,
     spread,
-    gate_rows,
     w_gate,
     w_up,
     w_down,
@@ -133,7 +133,7 @@
     for k in range(1, peers):
         pl.semaphore_signal(barrier, inc=1, device_id=in_plane(me + k), device_id_type=MESH)
     pl.semaphore_wait(barrier, planes - 1 + peers - 1)
-    for c in range(chunks):
+    for c in range(min(AHEAD, chunks)):
         for q in range(1, planes):
             z_copy(c, q).start()
 
@@ -166,6 +166,9 @@
     for c in range(chunks):
         for q in range(1, planes):
             z_copy(c, q).wait_recv()
+        if c + AHEAD < chunks:
+            for q in range(1, planes):
+                z_copy(c + AHEAD, q).start()
 
         def body(m, n, c=c):
             sent[c, m, n] = dot(pick[m, :], tokens[c, :, n]).astype(jnp.bfloat16)
@@ -199,8 +202,7 @@
         load_down(c).wait()
 
         def body(m, n, c=c):
-            y = dot(act[m, :], wd[c % 2, :, n]) * gate_rows[m, :]
-            sent[c, m, n] = y.astype(jnp.bfloat16)
+            sent[c, m, n] = dot(act[m, :], wd[c % 2, :, n]).astype(jnp.bfloat16)
 
         _tiles(rows, dc, mt, nt, body)
         if c + 2 < chunks:
@@ -227,10 +229,10 @@
             p_copy(c, q).wait_send()
 
 
-def moe(planes, ctx_n, slots, normed, residual, pick, spread, gate_rows, w_gate, w_up, w_down):
+def moe(planes, ctx_n, slots, normed, residual, pick, spread, w_gate, w_up, w_down):
     tok, width = normed.shape
     hid = w_gate.shape[2]
-    chunks = max(4, planes)
+    chunks = max(8, planes)
     peers = 2 * ctx_n
     rows = peers * slots
     dc = width // chunks
@@ -241,7 +243,7 @@
     return pl.pallas_call(
         functools.partial(_moe_kernel, dims),
         out_shape=jax.ShapeDtypeStruct((tok, width), jnp.bfloat16),
-        in_specs=[vmem] * 5 + [hbm] * 3,
+        in_specs=[vmem] * 4 + [hbm] * 3,
         out_specs=vmem,
         scratch_shapes=[
             pltpu.VMEM((chunks, planes * tok, dc), jnp.bfloat16),
@@ -269,7 +271,7 @@
         cost_estimate=pl.CostEstimate(
             flops=6 * rows * width * hid, bytes_accessed=6 * width * hid, transcendentals=rows * hid
         ),
-    )(normed, residual, pick, spread, gate_rows, w_gate, w_up, w_down)
+    )(normed, residual, pick, spread, w_gate, w_up, w_down)
 
 
 def slot_places(named, before, capacity):
@@ -293,25 +295,23 @@
     slots = _ceil(planes * capacity, 16)
     dp, cx = lax.axis_index("dp"), lax.axis_index("ctx")
     z, me = dp // 2, (dp % 2) * ctx_n + cx
-    ids = lax.all_gather(routes.T, ("dp", "ctx"), axis=0).reshape(planes, peers, TOP, tok)
-    gates = lax.all_gather(slot_gates.T, ("dp", "ctx"), axis=0).reshape(planes, peers, TOP, tok)
+    both = jnp.concatenate([routes.T.astype(jnp.float32), slot_gates.T])
+    column = [[2 * p + core for p in range(planes)] for core in range(2)]
+    both = lax.all_gather(both, "dp", axis=0, axis_index_groups=column)
+    both = countdown(both, z)
+    ids, gates = both[:, :TOP].astype(jnp.int32), both[:, TOP:]
     k = jnp.arange(peers, dtype=jnp.int32)
     row = jnp.arange(tok, dtype=jnp.int32)
     before = (row[:, None] < row[None, :]).astype(jnp.bfloat16)
     slot = jnp.arange(slots, dtype=jnp.int32)[None, :, None]
-    ids, gates = countdown(ids, z), countdown(gates, z)
-    mine = lax.dynamic_index_in_dim(ids, me, 1, keepdims=False)
     target = z * peers + (me + k) % peers
-    named = jnp.any(mine[None] == target[:, None, None, None], axis=2)
+    hit = ids[None] == target[:, None, None, None]
+    named = jnp.any(hit, axis=2)
+    gate = jnp.sum(jnp.where(hit, gates[None], 0.0), axis=2).reshape(peers, 1, planes * tok)
     pick = slot_places(named, before, capacity)[:, None, :] == slot
+    spread = jnp.where(pick, gate, 0.0).astype(jnp.bfloat16)
     pick = pick.astype(jnp.bfloat16).reshape(peers * slots, planes * tok)
-    hit = ids == z * peers + me
-    named = countdown(jnp.any(hit, axis=2).transpose(1, 0, 2), me)
-    gate = countdown(jnp.sum(jnp.where(hit, gates, 0.0), axis=2).transpose(1, 0, 2), me)
-    arrives = slot_places(named, before, capacity)[:, None, :] == slot
-    gate = gate.reshape(peers, 1, planes * tok)
-    gate_rows = jnp.sum(jnp.where(arrives, gate, 0.0), axis=2).reshape(peers * slots, 1)
-    return planes, ctx_n, slots, pick, pick.T, gate_rows
+    return planes, ctx_n, slots, pick, spread.reshape(peers * slots, planes * tok).T
 
 
 def local(
@@ -334,8 +334,8 @@
     ctx_index = lax.axis_index("ctx")
     query_rows = queries[0].reshape(tok_count, KVH, group_size, DH)
     query_pos = ctx_index * tok_count + jnp.arange(tok_count, dtype=jnp.int32)
-    key_piece = lax.all_gather(keys, "ctx", axis=1, tiled=True)
-    value_piece = lax.all_gather(values, "ctx", axis=1, tiled=True)
+    pair = lax.all_gather(jnp.concatenate([keys, values], 2), "ctx", axis=1, tiled=True)
+    key_piece, value_piece = jnp.split(pair, 2, axis=2)
     key_count = key_piece.shape[1]
     key_rows = key_piece[0].reshape(key_count, KVH, DH)
     value_rows = value_piece[0].reshape(key_count, KVH, DH)
@@ -377,7 +377,7 @@
     slot_gates = score_rows / jnp.sum(score_rows, axis=1, keepdims=True)
     expert_total = lax.axis_size(("dp", "ctx"))
     capacity = max(2, tok_count * TOP * 9 // (8 * expert_total))
-    planes, ctx_n, slots, pick, spread, gate_rows = tables(routes[0], slot_gates, capacity)
+    planes, ctx_n, slots, pick, spread = tables(routes[0], slot_gates, capacity)
     return moe(
         planes,
         ctx_n,
@@ -386,7 +386,6 @@
         residual,
         pick,
         spread,
-        gate_rows,
         gate_weight,
         up_weight,
         down_weight,

time: 492 us -> 380 us (0.77)
  blocking collectives: 151 us -> 24.8 us
  waiting for transfers between devices: 3.05 us -> 45.1 us
  Pallas kernels: 279 us -> 255 us
    all_gather x4 -> x2, blocking collectives: 151 us -> 24.8 us  [the longest x1 13.3 us: tables(): both = lax.all_gather(both, 'dp', axis=0, axis_index_groups=column)]
    all_gather x1, waiting for transfers between devices: 0.02 us -> 38.4 us  [local(): lax.all_gather(attended, 'ctx', axis=0, tiled=True)]
    pallas_call x1, Pallas kernels: 279 us -> 255 us  [moe(): pl.pallas_call(functools.partial(_moe_kernel, dims), out_shape=jax.ShapeD...]
  transfers between devices with their start and end apart: 2 -> 2, of which waited for: 1 -> 2; matrix products, arithmetic and copies ran while one was open for 2% -> 2% of each run, Pallas kernels for 0% -> 0%
where the time goes in v3:
time: 380 us
  Pallas kernels  255 us (67%)
  waiting for transfers between devices  45.1 us (12%)
  blocking collectives  24.8 us (7%)
  matrix products  15.5 us (4%)
  between operations  13.7 us (4%)
  local copies, waits for them, and re-layouts  13.4 us (4%)
  other arithmetic  7.28 us (2%)
  starting transfers between devices  4.43 us (1%)
    pallas_call x1, Pallas kernels, moe(): pl.pallas_call(functools.partial(_moe_kernel, dims), out_shape=jax.ShapeD...  255 us
    all_gather x1, waiting for transfers between devices, local(): lax.all_gather(attended, 'ctx', axis=0, tiled=True)  38.4 us
    all_gather x1, blocking collectives, tables(): both = lax.all_gather(both, 'dp', axis=0, axis_index_groups=column)  13.3 us
    all_gather x1, blocking collectives, local(): lax.all_gather(jnp.concatenate([keys, values], 2), 'ctx', axis=1, tiled=T...  11.5 us
    dot_general x1, matrix products, local(): jnp.dot(lax.all_gather(attended, 'ctx', axis=0, tiled=True), out_weight,...  10.1 us
  transfers between devices with their start and end apart: 2, of which 2 were waited for; matrix products, arithmetic and copies ran while one was open for 2% of the time, Pallas kernels for 0%

profile of v3, /device:TPU:0, one launch (start us, length us, event | category | flops | bytes accessed | tf_op | source)
XLA Modules:
  0.0 379.7 jit_solution(2362682795528621238)
XLA Ops:
  6.5 0.9 copy.36
  7.5 1.0 copy.35
  8.5 11.5 %all_gather.12 = bf16[1,512,512]{1,2,0:T(8,128)(2,1)S(1)} all-gather(bf16[1,128,512]{1,2,0:T(8,128)(2,1)S(1)} %pad_maximum_fusion), channel_id=1, replica_groups=mesh['dp'=8,'ctx'=4] {'ctx'}, dimensions={1}, use_global_device_ids=true | all-gather | bytes 655360 | tf_op jit(solution)/shard_map/all_gather | solution.py:337
  20.1 1.5 copy.52
  21.5 2.1 fusion
  23.6 2.1 fusion.1
  25.7 3.2 fusion.6
  28.9 0.0 all-gather.3.cloned.1.call-update
  29.0 13.3 %all-gather = f32[64,128]{1,0:T(8,128)S(1)} all-gather(f32[16,128]{1,0:T(8,128)S(1)} %pad_maximum_fusion.1), channel_id=2, replica_groups={{0,8,16,24},{4,12,20,28},{1,9,17,25},{5,13,21,29},{2,10,18,26},{6,14,22..., dimensions={0}, use_global_device_ids=true | all-gather | bytes 40960 | tf_op jit(solution)/shard_map/all_gather | solution.py:300
  42.4 0.1 fusion.15
  42.6 0.1 broadcast_in_dim.72
  42.7 0.7 copy.44
  43.4 0.1 compare_reduce_fusion
  43.5 38.4 %all-gather.3.cloned.1.call-done = bf16[512,4096]{0,1:T(8,128)(2,1)} async-done(((bf16[128,4096]{0,1:T(8,128)(2,1)}), bf16[512,4096]{0,1:T(8,128)(2,1)}) %all-gather.3.cloned.1.call-update) | async-done | bytes 4194320 | tf_op jit(solution)/shard_map/all_gather | solution.py:365
  82.0 10.1 %convolution_convert_fusion = bf16[512,1024]{1,0:T(8,128)(2,1)} fusion(bf16[512,4096]{0,1:T(8,128)(2,1)} %all-gather.3.cloned.1.call-done, bf16[4096,1024]{1,0:T(8,128)(2,1)} %param.15), kind=kOutput, calls=%fused_computation.14 | convolution fusion | flops 4295491584 | bytes 13631488 | tf_op jit(solution)/shard_map/dot_general | solution.py:364
  92.1 4.4 %all-to-all-start = ((bf16[4,128,1024]{2,1,0:T(8,128)(2,1)}), bf16[4,128,1024]{2,1,0:T(8,128)(2,1)}, u32[]{:S(2)}, u32[]{:S(2)}) async-start(bf16[4,128,1024]{2,1,0:T(8,128)(2,1)} %bitcast.10), calls=%async_computation | async-start | bytes 2097152 | tf_op jit(solution)/shard_map/all_to_all | solution.py:369
  96.5 0.1 fusion.12
  96.6 1.8 eq.44
  98.4 2.0 copy.43
  100.4 0.1 eq.47
  100.5 1.5 fusion.9
  102.1 0.1 convert_element_type.70
  102.2 1.4 copy.45.pick
  103.7 6.7 %all-to-all-done = bf16[4,128,1024]{2,1,0:T(8,128)(2,1)} async-done(((bf16[4,128,1024]{2,1,0:T(8,128)(2,1)}), bf16[4,128,1024]{2,1,0:T(8,128)(2,1)}, u32[]{:S(2)}, u32[]{:S(2)}) %all-to-all-start) | async-done | bytes 1048608 | tf_op jit(solution)/shard_map/all_to_all | solution.py:369
  110.3 1.5 convert_bitcast_fusion
  111.8 0.0 copy-start.2
  111.8 0.2 copy.51
  112.1 0.4 multiply_reduce_fusion
  112.5 1.3 copy-done
  113.9 1.3 multiply_convert_fusion.normed
  115.1 255.4 %shard_map.109 = bf16[128,4096]{1,0:T(8,128)(2,1)} custom-call(bf16[128,4096]{1,0:T(8,128)(2,1)} %multiply_convert_fusion.normed, f32[128,4096]{1,0:T(8,128)} %copy-done, bf16[1152,512]{1,0:T(8,128)(2,1)} %copy.45.pick, bf16[512,1152]{1,0:T(8,128)(2,1)} %get-tuple-element.5.spread, bf16[1,4096,768]{2,1,0:T(8,128)(2,1)} %w_gate.1, ...), custom_call_target="tpu_custom_call" | custom-call | flops 21743271936 | bytes 18874368 | tf_op jit(solution)/shard_map/pallas_call | solution.py:243
  370.6 2.3 copy.63
  (26 shorter events, 0.2 us)
Async XLA Ops:
  6.5 75.4 %all-gather.3.cloned.1.call-start = ((), (), s32[]{:S(2)}) async-start(), calls=%async_computation.1 | async-start | bytes 5242880 | tf_op jit(solution)/shard_map/all_gather | solution.py:365
  25.7 3.3 copy-start.3
  25.7 3.3 copy-start.4
  92.1 18.2 %all-to-all-start = ((bf16[4,128,1024]{2,1,0:T(8,128)(2,1)}), bf16[4,128,1024]{2,1,0:T(8,128)(2,1)}, u32[]{:S(2)}, u32[]{:S(2)}) async-start(bf16[4,128,1024]{2,1,0:T(8,128)(2,1)} %bitcast.10), calls=%async_computation | async-start | bytes 2097152 | tf_op jit(solution)/shard_map/all_to_all | solution.py:369
  103.6 8.4 %copy-start.1 = (bf16[1,128,4096]{2,1,0:T(8,128)(2,1)S(1)}, bf16[1,128,4096]{2,1,0:T(8,128)(2,1)}, u32[]{:S(2)}) copy-start(bf16[1,128,4096]{2,1,0:T(8,128)(2,1)} %param.11) | copy-start | bytes 3145732
  111.8 2.1 copy-start.2
  112.5 1.4 copy-start
Sparse Core Ops, SparseCore 0:
  29.1 52.8 all-gather.2
